TPU v7x, 32 devices: a whole 2x2x4 slice. The times are simulated.
32 devices in a mesh: rows: 8 (over z, x), seq: 4 (over y, core).
Axes of the slice: x: 2, y: 2, z: 4, core: 2. Of those that a mesh axis runs over, the one named last changes fastest.
Arguments:
- target: bfloat16 [16, 1024, 512], P('rows', 'seq'), may hold values from -6 to 6
- memory: bfloat16 [16, 1024, 512], P('rows', 'seq'), may hold values from -6 to 6
- target_segments: int32 [16, 1024], P('rows'), may hold values from 0 to 7, as said below
- memory_segments: int32 [16, 1024], P('rows'), may hold values from 0 to 7, as said below
- self_query: bfloat16 [512, 512], replicated, may hold values from -0.25 to 0.25
- self_key: bfloat16 [512, 512], replicated, may hold values from -0.25 to 0.25
- self_value: bfloat16 [512, 512], replicated, may hold values from -0.25 to 0.25
- self_output: bfloat16 [512, 512], replicated, may hold values from -1.5 to 1.5
- cross_query: bfloat16 [512, 512], replicated, may hold values from -0.25 to 0.25
- cross_key: bfloat16 [512, 512], replicated, may hold values from -0.25 to 0.25
- cross_value: bfloat16 [512, 512], replicated, may hold values from -0.25 to 0.25
- cross_output: bfloat16 [512, 512], replicated, may hold values from -1.5 to 1.5
- ffn_in: bfloat16 [512, 2048], replicated, may hold values from -0.25 to 0.25
- ffn_out: bfloat16 [2048, 512], replicated, may hold values from -0.125 to 0.125
- omega_self: float32 [512], replicated, may hold values from 0.5 to 2
- omega_cross: float32 [512], replicated, may hold values from 0.5 to 2
- omega_ffn: float32 [512], replicated, may hold values from 0.5 to 2
- gain_self: float32 [512], replicated, may hold values from 0.5 to 1.5
- bias_self: float32 [512], replicated, may hold values from -2.5 to 2.5
- gain_cross: float32 [512], replicated, may hold values from 0.5 to 1.5
- bias_cross: float32 [512], replicated, may hold values from -2.5 to 2.5
- gain_ffn: float32 [512], replicated, may hold values from 0.5 to 1.5
- bias_ffn: float32 [512], replicated, may hold values from -2.5 to 2.5
- cotangent: bfloat16 [16, 1024, 512], P('rows', 'seq'), may hold values from -6 to 6
Outputs:
- output: bfloat16 [16, 1024, 512], P('rows', 'seq')
- target_grad: float32 [16, 1024, 512], P('rows', 'seq')
- memory_grad: float32 [16, 1024, 512], P('rows', 'seq')
- self_query_grad: float32 [512, 512], replicated
- self_key_grad: float32 [512, 512], replicated
- self_value_grad: float32 [512, 512], replicated
- self_output_grad: float32 [512, 512], replicated
- cross_query_grad: float32 [512, 512], replicated
- cross_key_grad: float32 [512, 512], replicated
- cross_value_grad: float32 [512, 512], replicated
- cross_output_grad: float32 [512, 512], replicated
- ffn_in_grad: float32 [512, 2048], replicated
- ffn_out_grad: float32 [2048, 512], replicated
- omega_self_grad: float32 [512], replicated
- omega_cross_grad: float32 [512], replicated
- omega_ffn_grad: float32 [512], replicated
- gain_self_grad: float32 [512], replicated
- bias_self_grad: float32 [512], replicated
- gain_cross_grad: float32 [512], replicated
- bias_cross_grad: float32 [512], replicated
- gain_ffn_grad: float32 [512], replicated
- bias_ffn_grad: float32 [512], replicated
Inputs may be any that keep to these rules, and one draw needn't show every extreme that they name: `target_segments`: along each row the ids start at 0 and never fall. In each aligned block of 2 rows one row, drawn from the seed, is a single document; every other row holds exactly 8 documents of one or more positions. `memory_segments`: along each row the ids start at 0 and never fall, and a row holds exactly the document ids of the same row of target_segments, each at one or more positions.
All inputs are finite; a program needn't handle non-finite values.
Results may differ from a plain program's by a relative error of at most 0.034.
Values may be sent and summed in bfloat16 or wider, within the bound.
A program may use at most 256 MiB of HBM per device.

v0:
```python
import functools
import math
from types import SimpleNamespace
from typing import NamedTuple

import jax
import jax.numpy as jnp
from jax import lax
from jax.experimental import pallas as pl
from jax.experimental.pallas import tpu as pltpu
from jax.sharding import PartitionSpec as P

HEADS = 8


masked_score = -1e30


def from_behind(block, axis, distance):
    devices = range(lax.axis_size(axis))
    route = [(i - distance, i) for i in devices if i - distance in devices]
    return lax.ppermute(block, axis, route)


def shifted(block, axis, distance):
    devices = range(lax.axis_size(axis))
    route = [((i - distance) % len(devices), i) for i in devices]
    return lax.ppermute(block, axis, route)


def layer_norm(pre_norm, gain, bias):
    centred = pre_norm - jnp.mean(pre_norm, axis=-1, keepdims=True)
    spread = jnp.mean(centred * centred, axis=-1, keepdims=True)
    return centred * lax.rsqrt(spread + 1e-05) * gain + bias


def residual_norm(previous, branch, omega, gain, bias):
    return layer_norm(previous * omega + branch, gain, bias)


def forward_product(inputs, weight):
    return jnp.dot(inputs, weight, preferred_element_type=jnp.float32)


def weight_product(inputs, grads):
    return jnp.einsum("rsd,rsf->df", inputs, grads, preferred_element_type=jnp.float32)


def input_product(grads, weight):
    return jnp.einsum("rsf,df->rsd", grads, weight, preferred_element_type=jnp.float32)


def split_heads(values, head_count):
    return values.reshape(values.shape[0], values.shape[1], head_count, -1)


def attend_update(running, query_low, key_low, value_low, allowed, score_scale, head_count):
    best, total, accum = running
    raw = (
        jnp.einsum(
            "rqhe,rkhe->rqhk",
            split_heads(query_low, head_count),
            split_heads(key_low, head_count),
            preferred_element_type=jnp.float32,
        )
        * score_scale
    )
    scores = jnp.where(allowed[:, :, None, :], raw, masked_score)
    new_best = jnp.maximum(best, jnp.max(scores, axis=-1))
    weights = jnp.where(allowed[:, :, None, :], jnp.exp(scores - new_best[..., None]), 0.0)
    factor = jnp.exp(best - new_best)
    total = total * factor + jnp.sum(weights, axis=-1)
    accum = accum * factor[..., None] + jnp.einsum(
        "rqhk,rkhe->rqhe",
        weights.astype(jnp.bfloat16),
        split_heads(value_low, head_count),
        preferred_element_type=jnp.float32,
    )
    return (new_best, total, accum)


def attend_grads(
    query_low, key_low, value_low, grad_low, logsum, row_delta, allowed, score_scale, head_count
):
    query_heads = split_heads(query_low, head_count)
    key_heads = split_heads(key_low, head_count)
    value_heads = split_heads(value_low, head_count)
    grad_heads = split_heads(grad_low, head_count)
    raw = (
        jnp.einsum("rqhe,rkhe->rqhk", query_heads, key_heads, preferred_element_type=jnp.float32)
        * score_scale
    )
    scores = jnp.where(allowed[:, :, None, :], raw, masked_score)
    attention_weights = jnp.exp(scores - logsum[..., None])
    value_grad = jnp.einsum(
        "rqhk,rqhe->rkhe",
        attention_weights.astype(jnp.bfloat16),
        grad_heads,
        preferred_element_type=jnp.float32,
    )
    weight_grad = jnp.einsum(
        "rqhe,rkhe->rqhk", grad_heads, value_heads, preferred_element_type=jnp.float32
    )
    score_grad = (attention_weights * (weight_grad - row_delta[..., None])).astype(jnp.bfloat16)
    query_grad = (
        jnp.einsum("rqhk,rkhe->rqhe", score_grad, key_heads, preferred_element_type=jnp.float32)
        * score_scale
    )
    key_grad = (
        jnp.einsum("rqhk,rqhe->rkhe", score_grad, query_heads, preferred_element_type=jnp.float32)
        * score_scale
    )
    query_shape = (query_low.shape[0], query_low.shape[1], query_low.shape[2])
    key_shape = (key_low.shape[0], key_low.shape[1], key_low.shape[2])
    return (
        query_grad.reshape(query_shape),
        key_grad.reshape(key_shape),
        value_grad.reshape(key_shape),
    )


def ring_device(
    target,
    memory,
    target_segments,
    memory_segments,
    self_query,
    self_key,
    self_value,
    self_output,
    cross_query,
    cross_key,
    cross_value,
    cross_output,
    ffn_in,
    ffn_out,
    omega_self,
    omega_cross,
    omega_ffn,
    gain_self,
    bias_self,
    gain_cross,
    bias_cross,
    gain_ffn,
    bias_ffn,
    cotangent,
):
    batch_rows, local_span, model_width = target.shape
    head_count = HEADS
    head_width = model_width // head_count
    score_scale = 1.0 / math.sqrt(head_width)
    self_index = lax.axis_index("seq")
    axis_size = lax.axis_size("seq")
    offsets = jnp.arange(local_span, dtype=jnp.int32)
    local_ids = lax.dynamic_slice_in_dim(target_segments, self_index * local_span, local_span, 1)

    def block_mask(query_source, key_source):
        query_ids = lax.dynamic_slice_in_dim(
            target_segments, query_source * local_span, local_span, 1
        )
        key_ids = lax.dynamic_slice_in_dim(target_segments, key_source * local_span, local_span, 1)
        query_place = query_source * local_span + offsets
        key_place = key_source * local_span + offsets
        matching = query_ids[:, :, None] == key_ids[:, None, :]
        return matching & (key_place[None, None, :] <= query_place[None, :, None])

    empty_state = (
        jnp.full((batch_rows, local_span, head_count), masked_score, jnp.float32),
        jnp.zeros((batch_rows, local_span, head_count), jnp.float32),
        jnp.zeros((batch_rows, local_span, head_count, head_width), jnp.float32),
    )
    self_triple = jnp.concatenate((self_query, self_key, self_value), axis=1)
    triple_low = forward_product(target, self_triple).astype(jnp.bfloat16)
    query_low = triple_low[..., :model_width]
    key_low = triple_low[..., model_width : 2 * model_width]
    value_low = triple_low[..., 2 * model_width :]
    running = attend_update(
        empty_state,
        query_low,
        key_low,
        value_low,
        block_mask(self_index, self_index),
        score_scale,
        head_count,
    )

    def forward_turn(step_index, carry):
        key_pair, running = carry
        key_pair = from_behind((key_pair[0], key_pair[1]), "seq", 1)
        source = (self_index - step_index + axis_size) % axis_size

        def forward_visit(inner):
            return attend_update(
                inner,
                query_low,
                key_pair[0],
                key_pair[1],
                block_mask(self_index, source),
                score_scale,
                head_count,
            )

        running = lax.cond(source <= self_index, forward_visit, lambda inner: inner, running)
        return (key_pair, running)

    key_pair, running = lax.fori_loop(1, axis_size, forward_turn, ((key_low, value_low), running))
    best, total, accum = running
    self_logsum = best + jnp.log(total)
    self_heads = accum / total[..., None]
    self_low = self_heads.reshape(batch_rows, local_span, model_width).astype(jnp.bfloat16)
    self_branch = forward_product(self_low, self_output)
    target_wide = target.astype(jnp.float32)
    hidden_one, pull_one = jax.vjp(
        residual_norm, target_wide, self_branch, omega_self, gain_self, bias_self
    )
    hidden_one_low = hidden_one.astype(jnp.bfloat16)
    cross_query_low = forward_product(hidden_one_low, cross_query).astype(jnp.bfloat16)
    cross_pair = jnp.concatenate((cross_key, cross_value), axis=1)
    memory_pairs = forward_product(
        lax.all_gather(memory, "seq", axis=1, tiled=True), cross_pair
    ).astype(jnp.bfloat16)
    memory_total = memory_pairs.shape[1]
    key_block = 1024
    block_count = memory_total // key_block

    def cross_mask(block_index):
        key_ids = lax.dynamic_slice_in_dim(memory_segments, block_index * key_block, key_block, 1)
        return local_ids[:, :, None] == key_ids[:, None, :]

    def block_pairs(block_index):
        return lax.dynamic_slice_in_dim(memory_pairs, block_index * key_block, key_block, 1)

    def cross_turn(block_index, running):
        pairs = block_pairs(block_index)
        return attend_update(
            running,
            cross_query_low,
            pairs[..., :model_width],
            pairs[..., model_width:],
            cross_mask(block_index),
            score_scale,
            head_count,
        )

    best, total, accum = lax.fori_loop(0, block_count, cross_turn, empty_state)
    cross_logsum = best + jnp.log(total)
    cross_heads = accum / total[..., None]
    cross_low = cross_heads.reshape(batch_rows, local_span, model_width).astype(jnp.bfloat16)
    cross_branch = forward_product(cross_low, cross_output)
    hidden_two, pull_two = jax.vjp(
        residual_norm, hidden_one, cross_branch, omega_cross, gain_cross, bias_cross
    )
    hidden_two_low = hidden_two.astype(jnp.bfloat16)
    upward = forward_product(hidden_two_low, ffn_in)
    activated, pull_gelu = jax.vjp(jax.nn.gelu, upward)
    active_low = activated.astype(jnp.bfloat16)
    ffn_branch = forward_product(active_low, ffn_out)
    result, pull_three = jax.vjp(
        residual_norm, hidden_two, ffn_branch, omega_ffn, gain_ffn, bias_ffn
    )
    two_grad, ffn_branch_grad, omega_ffn_grad, gain_ffn_grad, bias_ffn_grad = pull_three(
        cotangent.astype(jnp.float32)
    )
    ffn_branch_low = ffn_branch_grad.astype(jnp.bfloat16)
    ffn_out_grad = weight_product(active_low, ffn_branch_low)
    upward_grad = pull_gelu(input_product(ffn_branch_low, ffn_out))[0]
    upward_low = upward_grad.astype(jnp.bfloat16)
    ffn_in_grad = weight_product(hidden_two_low, upward_low)
    two_grad = two_grad + input_product(upward_low, ffn_in)
    one_grad, cross_branch_grad, omega_cross_grad, gain_cross_grad, bias_cross_grad = pull_two(
        two_grad
    )
    cross_branch_low = cross_branch_grad.astype(jnp.bfloat16)
    cross_output_grad = weight_product(cross_low, cross_branch_low)
    cross_heads_grad = input_product(cross_branch_low, cross_output).astype(jnp.bfloat16)
    cross_delta = jnp.sum(
        split_heads(cross_heads_grad, head_count).astype(jnp.float32) * cross_heads, axis=-1
    )

    def cross_back(block_index, carry):
        query_grad, pair_grads = carry
        pairs = block_pairs(block_index)
        grads = attend_grads(
            cross_query_low,
            pairs[..., :model_width],
            pairs[..., model_width:],
            cross_heads_grad,
            cross_logsum,
            cross_delta,
            cross_mask(block_index),
            score_scale,
            head_count,
        )
        block_grads = jnp.concatenate((grads[1], grads[2]), axis=2)
        pair_grads = lax.dynamic_update_slice_in_dim(
            pair_grads, block_grads, block_index * key_block, 1
        )
        return (query_grad + grads[0], pair_grads)

    zero_grid = jnp.zeros((batch_rows, local_span, model_width), jnp.float32)
    cross_query_sum, pair_grads = lax.fori_loop(
        0,
        block_count,
        cross_back,
        (zero_grid, jnp.zeros((batch_rows, memory_total, 2 * model_width), jnp.float32)),
    )
    local_pair_grads = lax.psum_scatter(
        pair_grads.astype(jnp.bfloat16), "seq", scatter_dimension=1, tiled=True
    )
    memory_grad = input_product(local_pair_grads, cross_pair)
    pair_weight_grad = weight_product(memory, local_pair_grads)
    cross_query_low_grad = cross_query_sum.astype(jnp.bfloat16)
    cross_query_grad = weight_product(hidden_one_low, cross_query_low_grad)
    one_grad = one_grad + input_product(cross_query_low_grad, cross_query)
    target_residual_grad, self_branch_grad, omega_self_grad, gain_self_grad, bias_self_grad = (
        pull_one(one_grad)
    )
    self_branch_low = self_branch_grad.astype(jnp.bfloat16)
    self_output_grad = weight_product(self_low, self_branch_low)
    self_heads_grad = input_product(self_branch_low, self_output).astype(jnp.bfloat16)
    self_delta = jnp.sum(
        split_heads(self_heads_grad, head_count).astype(jnp.float32) * self_heads, axis=-1
    )

    def key_turn(step_index, carry):
        key_pair, grad_pair, query_grad = carry
        source = (self_index - step_index + axis_size) % axis_size

        def key_visit(inner):
            grads = attend_grads(
                query_low,
                key_pair[0],
                key_pair[1],
                self_heads_grad,
                self_logsum,
                self_delta,
                block_mask(self_index, source),
                score_scale,
                head_count,
            )
            return (inner[0] + grads[0], inner[1] + grads[1], inner[2] + grads[2])

        query_grad, key_grad, value_grad = lax.cond(
            source <= self_index,
            key_visit,
            lambda inner: inner,
            (query_grad, grad_pair[0], grad_pair[1]),
        )
        grad_pair = (
            shifted(key_grad.astype(jnp.bfloat16), "seq", 1).astype(key_grad.dtype),
            shifted(value_grad.astype(jnp.bfloat16), "seq", 1).astype(value_grad.dtype),
        )
        key_pair = from_behind((key_pair[0], key_pair[1]), "seq", 1)
        return (key_pair, grad_pair, query_grad)

    key_pair, grad_pair, query_grad = lax.fori_loop(
        0, axis_size, key_turn, ((key_low, value_low), (zero_grid, zero_grid), zero_grid)
    )
    key_grad, value_grad = grad_pair
    triple_grad_low = jnp.concatenate((query_grad, key_grad, value_grad), axis=2).astype(
        jnp.bfloat16
    )
    target_grad = target_residual_grad + input_product(triple_grad_low, self_triple)
    triple_weight_grad = weight_product(target, triple_grad_low)
    sums = lax.psum(
        (
            triple_weight_grad[:, :model_width],
            triple_weight_grad[:, model_width : 2 * model_width],
            triple_weight_grad[:, 2 * model_width :],
            self_output_grad,
            cross_query_grad,
            pair_weight_grad[:, :model_width],
            pair_weight_grad[:, model_width:],
            cross_output_grad,
            ffn_in_grad,
            ffn_out_grad,
            omega_self_grad,
            omega_cross_grad,
            omega_ffn_grad,
            gain_self_grad,
            bias_self_grad,
            gain_cross_grad,
            bias_cross_grad,
            gain_ffn_grad,
            bias_ffn_grad,
        ),
        ("rows", "seq"),
    )
    return (result.astype(jnp.bfloat16), target_grad, memory_grad) + tuple(sums)


MESH = pl.DeviceIdType.MESH
f32, bf16 = jnp.float32, jnp.bfloat16

def dot(a, b):
    return jnp.dot(a, b, preferred_element_type=f32)

def dot_t(a, b):
    return lax.dot_general(a, b, (((1,), (1,)), ((), ())), preferred_element_type=f32)

def t_dot(a, b):
    return lax.dot_general(a, b, (((0,), (0,)), ((), ())), preferred_element_type=f32)

def mult(i, m):
    return i if isinstance(i, int) else pl.multiple_of(i, m)

def attend_forward(first_block, blocks, keys, key, value_t, query_z, seen, scores, kept, kept_out, kept_sem, out_t, inverse, heads):
    count, piece, slots, queries = blocks * heads, 256, kept.shape[0], seen.shape[2]

    def head_place(i):
        block, head = first_block + i // heads, i % heads
        return block, head, pl.ds(mult(head * 64, 64), 64), pl.ds(mult(head // 2 * 128, 128), 128)

    def first(i, slot):
        block, head, _, pair = head_place(i)
        best = None
        for c in range(keys // piece):
            ks = pl.ds(c * piece, piece)
            s = dot(key[ks, pair], query_z[block, head]) + seen[block, ks]
            scores[slot, ks] = s
            top = jnp.max(s.reshape(piece // 8, 8, queries), axis=0)
            best = top if best is None else jnp.maximum(best, top)
        return best

    def out_copy(i):
        block, head, _, _ = head_place(i)
        return pltpu.make_async_copy(kept.at[i % slots, pl.ds(0, keys)], kept_out.at[block, head, pl.ds(0, keys)], kept_sem.at[i % slots])

    def second(i, slot, best):
        block, head, here, _ = head_place(i)
        best = jnp.max(best, axis=0, keepdims=True)
        total = out = None
        for c in range(keys // piece):
            ks = pl.ds(c * piece, piece)
            p = jnp.exp(scores[slot, ks] - best)
            part = jnp.sum(p.reshape(piece // 8, 8, queries), axis=0)
            total = part if total is None else total + part
            p = p.astype(bf16)
            kept[i % slots, ks] = p
            part = dot(value_t[here, ks], p)
            out = part if out is None else out + part
        scale = 1.0 / jnp.sum(total, axis=0, keepdims=True)
        out_t[block, here, :] = (out * scale).astype(bf16)
        inverse[block, head] = jnp.broadcast_to(scale, (8, queries))

    def body(j, best):
        i = 2 * j
        for e in range(2):
            pl.when(i + e >= slots)(lambda e=e: out_copy(i + e - slots).wait())
        later = first(i + 1, 1)
        second(i, 0, best)
        best = first(jnp.minimum(i + 2, count - 1), 0)
        second(i + 1, 1, later)
        out_copy(i).start()
        out_copy(i + 1).start()
        return best

    lax.fori_loop(0, count // 2, body, first(0, 0))
    for i in range(count - slots, count):
        out_copy(i).wait()

def norm_parts(pre):
    centred = pre - jnp.mean(pre, axis=-1, keepdims=True)
    rstd = lax.rsqrt(jnp.mean(centred * centred, axis=-1, keepdims=True) + 1e-05)
    return centred * rstd, rstd

def pad_pairs(query, query_z, row, heads):
    turned = query.T
    half = lax.broadcasted_iota(jnp.int32, (128, query.shape[0]), 0) // 64
    for head in range(heads):
        pair = turned[head // 2 * 128 : head // 2 * 128 + 128]
        query_z[row, head] = jnp.where(half == head % 2, pair, jnp.zeros_like(pair))

class ForwardIn(NamedTuple):
    target: object
    memory: object
    target_segments: object
    memory_segments: object
    self_query: object
    self_key: object
    self_value: object
    self_output: object
    cross_query: object
    cross_key: object
    cross_value: object
    cross_output: object
    ffn_in: object
    ffn_out: object
    omega_self: object
    omega_cross: object
    omega_ffn: object
    gain_self: object
    bias_self: object
    gain_cross: object
    bias_cross: object
    gain_ffn: object
    bias_ffn: object
    cotangent: object

class ForwardOut(NamedTuple):
    output_blocks: object
    target_all: object
    memory_all: object
    self_kept: object
    cross_kept: object
    self_inverse: object
    cross_inverse: object
    self_out: object
    cross_out: object
    self_q: object
    cross_q: object
    one_low: object
    one_hat: object
    one_rstd: object
    two_low: object
    two_hat: object
    two_rstd: object
    active: object
    upward_grad: object
    branch_grad: object
    two_grad: object
    sums: object

class ForwardScratch(NamedTuple):
    key: object
    value_t: object
    query_z: object
    seen_self: object
    seen_cross: object
    scores: object
    kept: object
    mem_key: object
    mem_value_t: object
    wide: object
    slope: object
    one: object
    two: object
    value_turned: object
    mem_value_turned: object
    grads: object

FORWARD_NAMES = ForwardIn._fields + ForwardOut._fields
MATRICES = ForwardIn._fields[4:14]
VECTORS = ForwardIn._fields[14:23]

def forward_kernel(heads, *refs):
    hbm = SimpleNamespace(**dict(zip(FORWARD_NAMES, refs)))
    own = refs[len(FORWARD_NAMES):-5]
    r = SimpleNamespace(**dict(zip(FORWARD_NAMES[2:4] + VECTORS + MATRICES + ForwardOut._fields + ForwardScratch._fields,
        refs[2:4] + refs[14:23] + own)))
    send, recv, local, load_sem, out_sem = refs[-5:]
    kept_sem = local
    me_r, me_s = lax.axis_index("rows"), lax.axis_index("seq")
    core, side = me_s % 2, me_s // 2
    length, width = r.target_all.shape
    tokens = r.one_low.shape[0]
    blocks = 2
    span = tokens // blocks
    other_core, other_side = me_s + 1 - 2 * core, me_s + 2 - 4 * side

    def place(i):
        return pl.ds(mult(i * span, span), span)

    def remote(src, dst, k, to):
        return pltpu.make_async_remote_copy(src_ref=src, dst_ref=dst, send_sem=send.at[k], recv_sem=recv.at[k],
            device_id=(me_r, to), device_id_type=MESH)

    def share(source, full, k):
        mine, theirs = full.at[place(me_s)], full.at[place(other_side)]
        return (pltpu.make_async_copy(source.at[side], mine, load_sem.at[10 + k // 3]), remote(source.at[1 - side], mine, k, other_side),
            remote(source.at[side], mine, k + 1, other_core), remote(theirs, theirs, k + 2, other_core))

    x_own, x_side, x_core, x_pass = share(hbm.target, r.target_all, 0)
    m_own, m_side, m_core, m_pass = share(hbm.memory, r.memory_all, 3)
    g_own = pltpu.make_async_copy(hbm.cotangent.at[side], r.grads.at[side], load_sem.at[12])
    g_side = remote(hbm.cotangent.at[1 - side], r.grads.at[side], 6, other_side)
    x_own.start()
    m_own.start()
    loads = {k: pltpu.make_async_copy(getattr(hbm, k), getattr(r, k), load_sem.at[i]) for i, k in enumerate(MATRICES)}
    for copy in loads.values():
        copy.start()
    g_own.start()
    loads = SimpleNamespace(**loads)
    outs = []

    def emit(*names):
        for k in names:
            copy = pltpu.make_async_copy(getattr(r, k), getattr(hbm, k), out_sem.at[len(outs)])
            copy.start()
            outs.append(copy)

    barrier = pltpu.get_barrier_semaphore()
    for to in (other_core, other_side):
        pl.semaphore_signal(barrier, inc=1, device_id=(me_r, to), device_id_type=MESH)
    pl.semaphore_wait(barrier, 2)
    x_side.start()
    x_core.start()
    m_core.start()

    def masks():
        def line(ids, at):
            first, second = ids[0:1, at], ids[1:2, at]
            return (first + (second - first) * side).astype(f32)
        mine = [line(r.target_segments, pl.ds(mult((2 * b + core) * span, span), span)) for b in range(blocks)]
        for c in range(length // 128):
            at = pl.ds(c * 128, 128)
            key_place = c * 128 + lax.broadcasted_iota(jnp.int32, (128, span), 0)
            query_place = lax.broadcasted_iota(jnp.int32, (128, span), 1)
            for ids, seen, causal in ((r.target_segments, r.seen_self, True), (r.memory_segments, r.seen_cross, False)):
                column = jnp.broadcast_to(line(ids, at), (128, 128)).T
                column = jnp.concatenate([column] * (span // 128), axis=1)
                for b in range(blocks):
                    if causal and c * 128 >= (b + 1) * length // 2:
                        continue
                    same = column == mine[b]
                    if causal:
                        same = same & (key_place <= query_place + (2 * b + core) * span)
                    seen[b, at] = jnp.where(same, 0.0, -1e30)

    def project(full, key_weight, turned, key, value_t, block):
        at = place(block)
        here = full[at]
        key[at] = dot(here, key_weight[...]).astype(bf16)
        value_t[:, at] = dot_t(turned[...], here).astype(bf16)

    def project_self(block):
        project(r.target_all, r.self_key, r.value_turned, r.key, r.value_t, block)

    def project_cross(block):
        project(r.memory_all, r.cross_key, r.mem_value_turned, r.mem_key, r.mem_value_t, block)

    def queries(low, weight, out):
        for b in range(blocks):
            query = (dot(low(b), weight[...]).astype(bf16) * 0.125).astype(bf16)
            out[b] = query
            pad_pairs(query, r.query_z, b, heads)

    masks()
    for k in (loads.self_query, loads.self_key, loads.self_value, loads.cross_key, loads.cross_value):
        k.wait()
    r.value_turned[...] = r.self_value[...].T
    r.mem_value_turned[...] = r.cross_value[...].T
    x_own.wait()
    project_self(me_s)
    x_core.wait()
    project_self(other_core)
    x_side.wait()
    x_pass.start()
    m_side.start()
    queries(lambda b: r.target_all[place(2 * b + core)], r.self_query, r.self_q)
    project_self(other_side)
    m_own.wait()
    project_cross(me_s)
    x_pass.wait()
    project_self(other_side + 1 - 2 * core)
    m_core.wait()
    project_cross(other_core)
    emit(*ForwardOut._fields[1:2], *ForwardOut._fields[9:10])

    def attend(first_block, count, keys, key, value_t, seen, kept_out, out_t, inverse):
        attend_forward(first_block, count, keys, key, value_t, r.query_z, seen, r.scores, r.kept, kept_out, kept_sem, out_t, inverse, heads)

    attend(0, 1, length // 2, r.key, r.value_t, r.seen_self, hbm.self_kept, r.self_out, r.self_inverse)
    m_side.wait()
    m_pass.start()
    g_side.start()
    attend(1, 1, length, r.key, r.value_t, r.seen_self, hbm.self_kept, r.self_out, r.self_inverse)
    loads.self_output.wait()
    vec = [getattr(r, k)[...].reshape(1, width) for k in VECTORS]
    part = 128
    for b in range(blocks):
        r.wide[pl.ds(b * span, span)] = t_dot(r.self_out[b], r.self_output[...])

    @pl.loop(0, tokens // part)
    def _(i):
        at = pl.ds(mult(i * part, part), part)
        b, inner = i // (span // part), i % (span // part)
        x = r.target_all[pl.ds(mult((2 * b + core) * span + inner * part, part), part)].astype(f32)
        hat, rstd = norm_parts(x * vec[0] + r.wide[at])
        one = hat * vec[3] + vec[4]
        r.one_hat[at] = hat
        r.one_rstd[at] = jnp.broadcast_to(rstd, (part, 128))
        r.one[at] = one
        r.one_low[at] = one.astype(bf16)

    loads.cross_query.wait()
    queries(lambda b: r.one_low[pl.ds(b * span, span)], r.cross_query, r.cross_q)
    project_cross(other_side)
    m_pass.wait()
    project_cross(other_side + 1 - 2 * core)
    emit(*ForwardOut._fields[2:3], *ForwardOut._fields[5:6], *ForwardOut._fields[7:8], *ForwardOut._fields[10:14])
    attend(0, 2, length, r.mem_key, r.mem_value_t, r.seen_cross, hbm.cross_kept, r.cross_out, r.cross_inverse)
    loads.cross_output.wait()
    for b in range(blocks):
        r.wide[pl.ds(b * span, span)] = t_dot(r.cross_out[b], r.cross_output[...])

    @pl.loop(0, tokens // part)
    def _(i):
        at = pl.ds(mult(i * part, part), part)
        hat, rstd = norm_parts(r.one[at] * vec[1] + r.wide[at])
        two = hat * vec[5] + vec[6]
        r.two_hat[at] = hat
        r.two_rstd[at] = jnp.broadcast_to(rstd, (part, 128))
        r.two[at] = two
        r.two_low[at] = two.astype(bf16)

    emit(*ForwardOut._fields[6:7], *ForwardOut._fields[8:9], *ForwardOut._fields[14:17])
    loads.ffn_in.wait()
    loads.ffn_out.wait()
    c0 = math.sqrt(2.0 / math.pi)
    pieces = r.ffn_in.shape[1] // 512
    r.wide[...] = jnp.zeros_like(r.wide)

    @pl.loop(0, pieces)
    def _(j):
        cols = pl.ds(mult(j * 512, 512), 512)
        for half in range(2):
            at = pl.ds(half * (tokens // 2), tokens // 2)
            u = dot(r.two_low[at], r.ffn_in[:, cols])
            square = u * u
            t = jnp.tanh(c0 * u * (1.0 + 0.044715 * square))
            active = (0.5 * u * (1.0 + t)).astype(bf16)
            r.active[at, cols] = active
            r.slope[at, cols] = (0.5 * (1.0 + t) + (0.5 * c0) * u * (1.0 - t * t) * (1.0 + (3 * 0.044715) * square)).astype(bf16)
            r.wide[at] += dot(active, r.ffn_out[cols, :])

    emit(*ForwardOut._fields[17:18])
    g_own.wait()
    g_side.wait()
    r.sums[...] = jnp.zeros_like(r.sums)

    @pl.loop(0, tokens // part)
    def _(i):
        at = pl.ds(mult(i * part, part), part)
        b, inner = i // (span // part), i % (span // part)
        near = pl.ds(mult(inner * part, part), part)
        two = r.two[at]
        hat, rstd = norm_parts(two * vec[2] + r.wide[at])
        r.output_blocks[b, near] = (hat * vec[7] + vec[8]).astype(bf16)
        grad = r.grads[b, near].astype(f32)
        scaled = grad * vec[7]
        back = rstd * (scaled - jnp.mean(scaled, axis=-1, keepdims=True) - hat * jnp.mean(scaled * hat, axis=-1, keepdims=True))
        r.branch_grad[at] = back.astype(bf16)
        r.two_grad[at] = back * vec[2]
        r.sums[0] += jnp.sum((back * two).reshape(part // 8, 8, width), axis=0)
        r.sums[1] += jnp.sum((grad * hat).reshape(part // 8, 8, width), axis=0)
        r.sums[2] += jnp.sum(grad.reshape(part // 8, 8, width), axis=0)

    emit(*ForwardOut._fields[:1], *ForwardOut._fields[19:])

    @pl.loop(0, pieces)
    def _(j):
        cols = pl.ds(mult(j * 512, 512), 512)
        for half in range(2):
            at = pl.ds(half * (tokens // 2), tokens // 2)
            grad = dot_t(r.branch_grad[at], r.ffn_out[cols, :])
            r.upward_grad[at, cols] = (grad * r.slope[at, cols].astype(f32)).astype(bf16)

    emit(*ForwardOut._fields[18:19])
    for copy in outs:
        copy.wait()

def forward_call(target, memory, target_segments, memory_segments, matrices, vectors, cotangent, heads=8):
    blocks, span, width = target.shape
    length = target_segments.shape[1]
    tokens = blocks * span
    hidden = matrices[8].shape[1]
    any_, vm = pl.BlockSpec(memory_space=pl.ANY), pl.BlockSpec(memory_space=pltpu.VMEM)
    s = jax.ShapeDtypeStruct
    full, wide, seen = ((length, width), bf16), ((tokens, width), f32), ((blocks, length, span), f32)
    kept, inverse = s((blocks, heads, length, span), bf16), s((blocks, heads, 8, span), f32)
    outs = ForwardOut(output_blocks=s((blocks, span, width), bf16), target_all=s(*full), memory_all=s(*full),
        self_kept=kept, cross_kept=kept, self_inverse=inverse, cross_inverse=inverse,
        self_out=s((blocks, width, span), bf16), cross_out=s((blocks, width, span), bf16),
        self_q=s((blocks, span, width), bf16), cross_q=s((blocks, span, width), bf16),
        one_low=s((tokens, width), bf16), one_hat=s(*wide), one_rstd=s((tokens, 128), f32),
        two_low=s((tokens, width), bf16), two_hat=s(*wide), two_rstd=s((tokens, 128), f32),
        active=s((tokens, hidden), bf16), upward_grad=s((tokens, hidden), bf16), branch_grad=s((tokens, width), bf16),
        two_grad=s(*wide), sums=s((3, 8, width), f32))
    turned = ((width, length), bf16)
    scratch = ForwardScratch(key=full, value_t=turned, query_z=((blocks, heads, 128, span), bf16),
        seen_self=seen, seen_cross=seen, scores=((2, length, span), f32),
        kept=((4, length, span), bf16), mem_key=full, mem_value_t=turned,
        wide=wide, slope=((tokens, hidden), bf16), one=wide, two=wide,
        value_turned=((width, width), bf16), mem_value_turned=((width, width), bf16), grads=((blocks, span, width), bf16))
    held = [((8, 128), f32) if k in ForwardOut._fields[3:5] else (o.shape, o.dtype) for k, o in zip(ForwardOut._fields, outs)]
    held = [(m.shape, m.dtype) for m in matrices] + held + list(scratch)
    dma = pltpu.SemaphoreType.DMA
    return ForwardOut(*pl.pallas_call(
        functools.partial(forward_kernel, heads),
        out_shape=list(outs),
        in_specs=[any_] * 2 + [vm] * 2 + [any_] * 10 + [vm] * 9 + [any_],
        out_specs=[any_] * len(outs),
        scratch_shapes=[pltpu.VMEM(*k) for k in held] + [dma((7,)), dma((7,)), dma((4,)), dma((13,)), dma((20,))],
        compiler_params=pltpu.CompilerParams(collective_id=0, has_side_effects=True, vmem_limit_bytes=62 << 20),
        name="forward",
    )(target, memory, target_segments, memory_segments, *matrices, *vectors, cotangent))

CLASSES = (1, 4, 0, 1, 4, 4, 0, 5, 1, 4, 1, 1, 3, 0, 1, 0)
PLAN = (
    (0,),
    (19, 1),
    (),
    (),
    (2, 4),
    (0,),
    (1, 3, 6),
    (7,),
    (2, 4, 3, 6, 7),
    (19, 1, 5),
    (),
    (),
    (),
    (2, 1, 5, 0),
    (4, 3),
    (7, 1, 6),
    (2, 4, 8, 1),
    (5,),
    (7, 6),
    (0, 1, 2, 8),
    (16, 4, 9, 3),
    (),
    (18, 5, 11, 7, 10),
    (12,),
    (6,),
    (16, 8, 18, 7, 4, 9, 1, 2, 11, 0, 10, 3),
    (12, 7, 5, 8, 6),
    (2, 1, 3, 0),
    (9,),
    (16, 18, 4, 12),
    (7, 13),
    (1, 8),
    (14, 6),
    (17, 18, 2, 3, 1, 13, 11, 14, 0),
    (15, 9, 10, 5, 4, 17, 2, 15, 12, 13, 7, 8, 14, 6, 5, 11, 18, 10, 3, 0, 9, 2, 4, 8, 17, 5, 12, 11, 2, 15, 18, 13, 10, 14, 8, 3, 5, 7, 11, 0, 13, 6, 10, 9, 14, 7, 11, 15, 4, 13, 12, 10, 14, 8, 11, 4, 3, 15, 13, 10, 14, 5, 3, 15, 0, 13, 9, 14, 5, 6, 0, 15, 12, 8, 9, 11, 6, 13, 15, 12, 10, 8, 14, 9, 11, 13, 15, 12, 11, 13, 9, 10, 9, 12, 15, 10, 14, 12, 15, 14),
)

class Reduction:
    def __init__(self, block, near, landed, reduced, send, recv, own):
        self.block, self.near, self.landed, self.reduced = block, near, landed, reduced
        self.send, self.recv, self.own = send, recv, own
        self.r, self.s = lax.axis_index("rows"), lax.axis_index("seq")
        self.core, self.y = self.s % 2, self.s // 2
        self.x, self.z0, self.z1 = self.r % 2, (self.r // 2) % 2, self.r // 4
        self.count, self.size = block.shape[0], block.shape[1]
        x, y, z0, z1 = self.x, self.y, self.z0, self.z1
        core, ax, ay = (0, 1 - 2 * self.core, self.core), (1 - 2 * x, 0, x), (0, 2 - 4 * y, y)
        an, af = (2 - 4 * z0, 0, z0), (4 - 8 * z1, 0, z1)
        self.orders = ((core, ax, ay, an, af), (core, ay, ax, an, af), (core, an, af, ax, ay), (core, an, af, ay, ax), (core, ax, an, af, ay), (core, ay, an, af, ax))
        self.flows, self.turn, done = {}, 0, {}
        self.polls = []
        for entry in PLAN:
            self.polls.append([(c, done.setdefault(c, []).append(0) or len(done[c]) - 1) for c in entry])

    def partners(self):
        r, s = self.r, self.s
        return ((r, s + 1 - 2 * self.core), (r, s + 2 - 4 * self.y), (r + 1 - 2 * self.x, s),
                (r + 2 - 4 * self.z0, s), (r + 4 - 8 * self.z1, s))

    def start_of(self, j, hops):
        off = 0
        for i in range(j):
            off = off + hops[i][2] * (self.size >> (i + 1))
        return off

    def landing(self, c, j):
        half = self.size >> (j + 1)
        if j == 0:
            return self.near.at[c]
        return self.landed.at[c, pl.ds(self.size // 2 - (self.size >> j), half)]

    def copy(self, c, j, gather):
        hops = self.orders[CLASSES[c]]
        off, half = self.start_of(j, hops), self.size >> (j + 1)
        dr, ds, bit = hops[j]
        if gather:
            mine = pl.ds(pl.multiple_of(off + bit * half, 16), half)
            src, dst = (self.block if j == 4 else self.reduced).at[c, mine], self.reduced.at[c, mine]
        else:
            src, dst = self.block.at[c, pl.ds(pl.multiple_of(off + (1 - bit) * half, 16), half)], self.landing(c, j)
        return pltpu.make_async_remote_copy(src_ref=src, dst_ref=dst, send_sem=self.send.at[c],
            recv_sem=self.recv.at[c, j + 5 * gather], device_id=(self.r + dr, self.s + ds), device_id_type=MESH)

    def own_copy(self, c):
        mine = pl.ds(pl.multiple_of(self.start_of(5, self.orders[CLASSES[c]]), 16), self.size >> 5)
        return pltpu.make_async_copy(self.block.at[c, mine], self.reduced.at[c, mine], self.own.at[c])

    def add(self, c, j):
        keep = pl.ds(pl.multiple_of(self.start_of(j + 1, self.orders[CLASSES[c]]), 16), self.size >> (j + 1))
        self.block[c, keep] = (self.block[c, keep].astype(f32) + self.landing(c, j)[...].astype(f32)).astype(bf16)

    def step(self, c, s):
        if c >= self.count:
            return self.flows[c](s)
        if 1 <= s <= 5:
            self.copy(c, s - 1, 0).wait()
            self.add(c, s - 1)
        elif s > 5:
            self.copy(c, 10 - s, 1).wait()
        if s == 5:
            self.own_copy(c).start()
        elif s == 6:
            self.own_copy(c).wait()
        if s <= 4:
            self.copy(c, s, 0).start()
        elif s <= 9:
            self.copy(c, 9 - s, 1).start()

    def poll(self, index=None):
        if index is None:
            index = self.turn
            self.turn += 1
        for c, s in self.polls[index]:
            self.step(c, s)

    def poll_loop(self, base, count, i):
        for k in range(count):
            if self.polls[base + k]:
                @pl.when(i == k)
                def _():
                    self.poll(base + k)

class Loads(NamedTuple):
    active: object
    branch_grad: object
    two_low: object
    upward_grad: object
    ffn_in: object
    two_grad: object
    two_hat: object
    two_rstd: object
    one_hat: object
    one_rstd: object
    cross_output: object
    cross_out: object
    cross_inverse: object
    memory_all: object
    cross_key: object
    cross_value: object
    cross_q: object
    one_low: object
    cross_query: object
    target_all: object
    self_output: object
    self_out: object
    self_inverse: object
    self_key: object
    self_value: object
    self_q: object
    self_query: object
    sums: object

class BackOut(NamedTuple):
    output: object
    reduced: object
    target_grad: object
    memory_grad: object
    vector_grads: object

class BackScratch(NamedTuple):
    block: object
    near: object
    landed: object
    key_t: object
    value: object
    key_grad: object
    value_grad: object
    score_grad: object
    kept: object
    part: object
    part_core: object
    part_side: object
    query_grad_t: object
    query_grad: object
    branch_low: object
    out_grad_t: object
    out_grad: object
    delta: object
    vec: object
    vec_landed: object
    acc: object
    output_own: object

LOADS = Loads._fields
UNLOADED = ForwardOut._fields[3:5] + ForwardOut._fields[:1] + VECTORS

def backward_kernel(heads, *refs):
    n = len(LOADS + UNLOADED)
    hbm = SimpleNamespace(**dict(zip(LOADS + UNLOADED, refs)))
    r = SimpleNamespace(**dict(zip(BackOut._fields + LOADS + BackScratch._fields, refs[n:])))
    load_sem, kept_sem, send, recv, own_sem, part_send, part_recv, vec_send, vec_recv, out_sem = refs[-10:]
    length, width = r.memory_all.shape
    tokens = r.two_low.shape[0]
    blocks = 2
    span = tokens // blocks
    red = Reduction(r.block, r.near, r.landed, r.reduced, send, recv, own_sem)
    me_r, me_s, core, side = red.r, red.s, red.core, red.y

    loads = Loads(*[pltpu.make_async_copy(getattr(hbm, k), getattr(r, k), load_sem.at[i]) for i, k in enumerate(LOADS)])
    for copy in loads:
        copy.start()

    def need(*copies):
        for copy in copies:
            copy.wait()

    barrier = pltpu.get_barrier_semaphore()
    for to in red.partners():
        pl.semaphore_signal(barrier, inc=1, device_id=to, device_id_type=MESH)
    pl.semaphore_wait(barrier, 5)

    def block_at(b):
        return pl.ds(b * span, span)

    def place(i):
        return pl.ds(mult(i * span, span), span)

    def ffn_block(c):
        if c < 4:
            r.block[c] = t_dot(r.active[:, pl.ds(c * 512, 512)], r.branch_grad[...]).astype(bf16)
        else:
            r.block[c] = t_dot(r.two_low[...], r.upward_grad[:, pl.ds((c - 4) * 512, 512)]).astype(bf16)

    vec = [getattr(hbm, k)[...].reshape(1, width) for k in VECTORS]
    part = 128

    def norm_back(grad_ref, hat_ref, rstd_ref, gain, omega, previous, slot):
        for i in range(3):
            r.acc[slot + i] = jnp.zeros_like(r.acc[slot + i])

        @pl.loop(0, tokens // part)
        def _(i):
            at = pl.ds(mult(i * part, part), part)
            hat, grad = hat_ref[at], grad_ref[at]
            scaled = grad * gain
            back = rstd_ref[at][:, 0:1] * (scaled - jnp.mean(scaled, axis=-1, keepdims=True)
                - hat * jnp.mean(scaled * hat, axis=-1, keepdims=True))
            r.branch_low[at] = back.astype(bf16)
            grad_ref[at] = back * omega
            for k, term in enumerate((back * previous(i), grad * hat, grad)):
                r.acc[slot + k] += jnp.sum(term.reshape(part // 8, 8, width), axis=0)

    def attention_start(weight, out_t, inverse):
        for b in range(blocks):
            grad_t = dot_t(weight[...], r.branch_low[block_at(b)])
            for head in range(heads):
                here = pl.ds(head * 64, 64)
                scaled = grad_t[head * 64 : head * 64 + 64] * inverse[b, head][0:1]
                r.out_grad_t[b, here] = scaled.astype(bf16)
                delta = jnp.sum(scaled * out_t[b, here].astype(f32), axis=0, keepdims=True)
                r.delta[b, head] = jnp.broadcast_to(delta, (8, span))
            r.out_grad[b] = r.out_grad_t[b].T

    def keys_again(full, key_weight, value_weight):
        key_turned = key_weight[...].T
        for c in range(length // 512):
            at = pl.ds(c * 512, 512)
            here = full[at]
            r.key_t[:, at] = dot_t(key_turned, here).astype(bf16)
            r.value[at] = dot(here, value_weight[...]).astype(bf16)

    def attention_back(kept_hbm, query, spans):
        base = red.turn
        pairs, piece = heads // 2, 256
        red.turn += pairs
        tiles = [(b, e) for b in range(blocks) for e in range(2)]
        top = lax.broadcasted_iota(jnp.int32, (128, span), 0) // 64
        left = lax.broadcasted_iota(jnp.int32, (span, 128), 1) // 64

        def pair_at(j):
            return pl.ds(mult(j * 128, 128), 128)

        def fetch(j, b, e):
            slot, ks = j % 3 * 4 + b * 2 + e, pl.ds(0, spans[b])
            return pltpu.make_async_copy(kept_hbm.at[b, 2 * j + e, ks], r.kept.at[slot, ks], kept_sem.at[slot])

        def first(j):
            for b, e in tiles:
                fetch(j, b, e).wait()
            for b, e in tiles:
                grad = jnp.where(top == e, r.out_grad_t[b, pair_at(j), :], jnp.zeros((128, span), bf16))
                delta = r.delta[b, 2 * j + e][0:1]
                for c in range(spans[b] // piece):
                    ks = pl.ds(c * piece, piece)
                    p_grad = dot(r.value[ks, pair_at(j)], grad)
                    r.score_grad[j % 2 * 4 + b * 2 + e, ks] = (r.kept[j % 3 * 4 + b * 2 + e, ks].astype(f32) * (p_grad - delta)).astype(bf16)

        def second(j):
            none = jnp.zeros((span, 128), bf16)
            qs = [jnp.where(left == e, query[b, :, pair_at(j)], none) for b, e in tiles]
            gs = [jnp.where(left == e, r.out_grad[b, :, pair_at(j)], none) for b, e in tiles]
            out = [None] * len(tiles)
            for c in range(length // piece):
                ks = pl.ds(c * piece, piece)
                v_grad = k_grad = None
                for i, (b, e) in enumerate(tiles):
                    if c * piece >= spans[b]:
                        continue
                    ds = r.score_grad[j % 2 * 4 + i, ks]
                    v, k = dot(r.kept[j % 3 * 4 + i, ks], gs[i]), dot(ds, qs[i])
                    v_grad, k_grad = (v, k) if v_grad is None else (v_grad + v, k_grad + k)
                    a = dot(r.key_t[pl.ds(mult(j * 128 + e * 64, 64), 64), ks], ds)
                    out[i] = a if out[i] is None else out[i] + a
                r.value_grad[ks, pair_at(j)] = v_grad.astype(bf16)
                r.key_grad[ks, pair_at(j)] = k_grad.astype(bf16)
            for i, (b, e) in enumerate(tiles):
                r.query_grad_t[b, pl.ds(mult(j * 128 + e * 64, 64), 64), :] = (out[i] * 0.125).astype(bf16)

        for j in range(2):
            for b, e in tiles:
                fetch(j, b, e).start()
        first(0)

        @pl.loop(0, pairs - 1)
        def _(j):
            @pl.when(j + 2 < pairs)
            def _():
                for b, e in tiles:
                    fetch(j + 2, b, e).start()
            first(j + 1)
            second(j)
            red.poll_loop(base, pairs - 1, j)
        second(pairs - 1)
        red.poll(base + pairs - 1)
        for b in range(blocks):
            r.query_grad[b] = r.query_grad_t[b].T

    def pair_product(key_weight, value_weight):
        for i in range(length // span):
            at = block_at(i)
            r.part[i] = (dot_t(r.key_grad[at], key_weight[...]) + dot_t(r.value_grad[at], value_weight[...])).astype(bf16)

    def part_copy(k, src, dst, to):
        return pltpu.make_async_remote_copy(src_ref=src, dst_ref=dst, send_sem=part_send.at[k], recv_sem=part_recv.at[k],
            device_id=(me_r, to), device_id_type=MESH)

    def part_flow(turn, out, rest):
        to_core, to_side = me_s + 1 - 2 * core, me_s + 2 - 4 * side
        far, near = 1 - side, side
        copies = (part_copy(3 * turn, r.part.at[2 * far + 1 - core], r.part_core.at[turn, 0], to_core),
            part_copy(3 * turn + 1, r.part.at[2 * near + 1 - core], r.part_core.at[turn, 1], to_core),
            part_copy(3 * turn + 2, r.part_core.at[turn, 0], r.part_side.at[turn], to_side))

        def step(s):
            if s == 0:
                copies[0].start()
                copies[1].start()
            elif s == 1:
                copies[0].wait()
                r.part_core[turn, 0] = (r.part[2 * far + core].astype(f32) + r.part_core[turn, 0].astype(f32) + rest(far)).astype(bf16)
                copies[2].start()
                copies[1].wait()
                out[near] = r.part[2 * near + core].astype(f32) + r.part_core[turn, 1].astype(f32) + rest(near)
            else:
                copies[2].wait()
                out[far] = r.part_side[turn].astype(f32)
        return step

    def output_flow(s):
        there = pltpu.make_async_remote_copy(src_ref=hbm.output_blocks.at[1 - side], dst_ref=r.output.at[side], send_sem=part_send.at[6],
            recv_sem=part_recv.at[6], device_id=(me_r, me_s + 2 - 4 * side), device_id_type=MESH)
        if s == 0:
            there.start()
            pltpu.make_async_copy(hbm.output_blocks.at[side], r.output_own, out_sem.at[0]).start()
        else:
            there.wait()
            pltpu.make_async_copy(hbm.output_blocks.at[side], r.output_own, out_sem.at[0]).wait()
            pltpu.make_async_copy(r.output_own, r.output.at[side], out_sem.at[1]).start()

    def vec_copy(k):
        return pltpu.make_async_remote_copy(src_ref=r.vec, dst_ref=r.vec_landed.at[k], send_sem=vec_send.at[k],
            recv_sem=vec_recv.at[k], device_id=red.partners()[k], device_id_type=MESH)

    def vec_flow(s):
        if s >= 1:
            vec_copy(s - 1).wait()
            r.vec[...] += r.vec_landed[s - 1]
        if s <= 4:
            vec_copy(s).start()
        else:
            r.vector_grads[...] = r.vec[...]

    red.flows = {16: part_flow(0, r.memory_grad, lambda b: 0.0), 18: vec_flow, 19: output_flow,
        17: part_flow(1, r.target_grad, lambda b: r.two_grad[place(b)])}

    need(loads.active, loads.branch_grad)
    for c in range(8):
        if c == 4:
            need(loads.two_low, loads.upward_grad)
        ffn_block(c)
        red.poll()
    need(loads.ffn_in, loads.two_grad)

    @pl.loop(0, tokens // 128)
    def _(i):
        at = pl.ds(mult(i * 128, 128), 128)
        r.two_grad[at] += dot_t(r.upward_grad[at], r.ffn_in[...])
    red.poll()
    need(loads.two_hat, loads.two_rstd, loads.one_hat, loads.one_rstd, loads.cross_output, loads.cross_out, loads.cross_inverse)
    norm_back(r.two_grad, r.two_hat, r.two_rstd, vec[5], vec[1], lambda i: r.one_hat[pl.ds(mult(i * part, part), part)] * vec[3] + vec[4], 0)
    red.poll()
    r.block[8] = sum(dot(r.cross_out[b], r.branch_low[block_at(b)]) for b in range(blocks)).astype(bf16)
    red.poll()
    attention_start(r.cross_output, r.cross_out, r.cross_inverse)
    red.poll()
    need(loads.memory_all, loads.cross_key, loads.cross_value, loads.cross_q)
    keys_again(r.memory_all, r.cross_key, r.cross_value)
    red.poll()
    attention_back(hbm.cross_kept, r.cross_q, (length, length))
    r.block[9] = t_dot(r.memory_all[...], r.key_grad[...]).astype(bf16)
    red.poll()
    r.block[10] = t_dot(r.memory_all[...], r.value_grad[...]).astype(bf16)
    red.poll()
    need(loads.one_low, loads.cross_query)
    r.block[11] = sum(t_dot(r.one_low[block_at(b)], r.query_grad[b]) for b in range(blocks)).astype(bf16)
    red.poll()
    pair_product(r.cross_key, r.cross_value)
    red.poll()
    for b in range(blocks):
        r.two_grad[block_at(b)] += dot_t(r.query_grad[b], r.cross_query[...])
    red.poll()
    need(loads.target_all, loads.self_output, loads.self_out, loads.self_inverse, loads.self_key, loads.self_value, loads.self_q,
        loads.self_query, loads.sums)
    def own_target(i):
        b, inner = i // (span // part), i % (span // part)
        return r.target_all[pl.ds(mult((2 * b + core) * span + inner * part, part), part)].astype(f32)
    norm_back(r.two_grad, r.one_hat, r.one_rstd, vec[3], vec[0], own_target, 3)
    for i in range(3):
        r.vec[pl.ds(i, 1)] = jnp.sum(r.acc[3 + i], axis=0, keepdims=True)
        r.vec[pl.ds(3 + i, 1)] = jnp.sum(r.acc[i], axis=0, keepdims=True)
        r.vec[pl.ds(6 + i, 1)] = jnp.sum(r.sums[i], axis=0, keepdims=True)
    r.vec[pl.ds(9, 7)] = jnp.zeros((7, width), f32)
    red.poll()
    r.block[12] = sum(dot(r.self_out[b], r.branch_low[block_at(b)]) for b in range(blocks)).astype(bf16)
    red.poll()
    attention_start(r.self_output, r.self_out, r.self_inverse)
    red.poll()
    keys_again(r.target_all, r.self_key, r.self_value)
    red.poll()
    attention_back(hbm.self_kept, r.self_q, (length // 2, length))
    r.block[13] = t_dot(r.target_all[...], r.key_grad[...]).astype(bf16)
    red.poll()
    r.block[14] = t_dot(r.target_all[...], r.value_grad[...]).astype(bf16)
    red.poll()
    r.block[15] = sum(t_dot(r.target_all[place(2 * b + core)], r.query_grad[b]) for b in range(blocks)).astype(bf16)
    red.poll()
    pair_product(r.self_key, r.self_value)
    for b in range(blocks):
        r.two_grad[block_at(b)] += dot_t(r.query_grad[b], r.self_query[...])
    red.poll()
    red.poll()
    pltpu.make_async_copy(r.output_own, r.output.at[side], out_sem.at[1]).wait()

def backward_call(o, matrices, vectors, heads=8):
    length, width = o.target_all.shape
    tokens, hidden = o.active.shape
    blocks = o.self_kept.shape[0]
    span = tokens // blocks
    any_, vm = pl.BlockSpec(memory_space=pl.ANY), pl.BlockSpec(memory_space=pltpu.VMEM)
    s = jax.ShapeDtypeStruct
    operands = dict(o._asdict(), **dict(zip(MATRICES + VECTORS, matrices + vectors)))
    count = 8 + 2 * hidden // 512
    outs = BackOut(output=s((blocks, span, width), bf16), reduced=s((count, 512, width), bf16), target_grad=s((blocks, span, width), f32),
        memory_grad=s((blocks, span, width), f32), vector_grads=s((16, width), f32))
    full, near, block = ((length, width), bf16), ((blocks, span, width), bf16), ((blocks, width, span), bf16)
    scratch = BackScratch(block=((count, 512, width), bf16), near=((count, 256, width), bf16), landed=((count, 256, width), bf16),
        key_t=((width, length), bf16), value=full, key_grad=full, value_grad=full,
        score_grad=((8, length, span), bf16), kept=((12, length, span), bf16), part=((length // span, span, width), bf16),
        part_core=((2, 2, span, width), bf16), part_side=((2, span, width), bf16),
        query_grad_t=block, query_grad=near, branch_low=((tokens, width), bf16),
        out_grad_t=block, out_grad=near, delta=((blocks, heads, 8, span), f32),
        vec=((16, width), f32), vec_landed=((5, 16, width), f32), acc=((6, 8, width), f32), output_own=((span, width), bf16))
    dma = pltpu.SemaphoreType.DMA
    return BackOut(*pl.pallas_call(
        functools.partial(backward_kernel, heads),
        out_shape=list(outs),
        in_specs=[vm if k in VECTORS else any_ for k in LOADS + UNLOADED],
        out_specs=[any_, any_, vm, vm, vm],
        scratch_shapes=[pltpu.VMEM(operands[k].shape, operands[k].dtype) for k in LOADS] + [pltpu.VMEM(*k) for k in scratch]
            + [dma((len(LOADS),)), dma((12,)), dma((count,)), dma((count, 10)), dma((count,)), dma((7,)), dma((7,)), dma((5,)), dma((5,)), dma((2,))],
        compiler_params=pltpu.CompilerParams(collective_id=1, has_side_effects=True, vmem_limit_bytes=63 << 20),
        name="backward",
    )(*(operands[k] for k in LOADS + UNLOADED)))

FINISH_BLOCK = (15, 13, 14, 12, 11, 9, 10, 8)
VECTOR_PLACE = (0, 3, 6, 1, 2, 4, 5, 7, 8)

def finish_kernel(reduced, vector_grads, output, target_grad, memory_grad, *refs):
    outs, small, handed = refs[3:13], refs[13:22], refs[:3]
    low, vec, stage, *between, load_sem, store_sem, sem = refs[22:]
    slots, count = stage.shape[0], reduced.shape[0]
    wide = outs[8].shape[1] // 512
    places = [outs[9].at[pl.ds(512 * i, 512)] for i in range(wide)] + [outs[8].at[:, pl.ds(512 * i, 512)] for i in range(wide)]
    places += [None] * 8
    for out, block in zip(outs, FINISH_BLOCK):
        places[block] = out
    loads = [pltpu.make_async_copy(reduced.at[i], low.at[i], load_sem.at[i]) for i in range(count)]
    for copy in loads:
        copy.start()
    arrive = [pltpu.make_async_copy(a, b, sem.at[i]) for i, (a, b) in enumerate(zip((output, target_grad, memory_grad, vector_grads), (*between, vec)))]
    leave = [pltpu.make_async_copy(a, b, sem.at[4 + i]) for i, (a, b) in enumerate(zip(between, handed))]
    for copy in arrive:
        copy.start()
    copies = [pltpu.make_async_copy(stage.at[i % slots], place, store_sem.at[i % slots]) for i, place in enumerate(places)]
    for i, copy in enumerate(copies):
        if i >= slots:
            copies[i - slots].wait()
        loads[i].wait()
        stage[i % slots] = low[i].astype(f32)
        copy.start()
    for copy in arrive:
        copy.wait()
    for copy in leave:
        copy.start()
    for ref, row in zip(small, VECTOR_PLACE):
        ref[...] = vec[row]
    for copy in copies[-slots:] + leave:
        copy.wait()

def finish_call(back, hidden):
    count, rows, width = back.reduced.shape
    any_, vm = pl.BlockSpec(memory_space=pl.ANY), pl.BlockSpec(memory_space=pltpu.VMEM)
    s = jax.ShapeDtypeStruct
    handed = [back.output, back.target_grad, back.memory_grad]
    shapes = [s(a.shape, a.dtype) for a in handed] + [s((width, width), f32)] * 8 + [s((width, hidden), f32), s((hidden, width), f32)]
    dma = pltpu.SemaphoreType.DMA
    return pl.pallas_call(
        finish_kernel,
        out_shape=shapes + [s((width,), f32)] * 9,
        in_specs=[any_] * 5,
        out_specs=[any_] * 13 + [vm] * 9,
        scratch_shapes=[pltpu.VMEM(back.reduced.shape, bf16), pltpu.VMEM((16, width), f32), pltpu.VMEM((8, rows, width), f32)]
            + [pltpu.VMEM(a.shape, a.dtype) for a in handed] + [dma((count,)), dma((8,)), dma((7,))],
        compiler_params=pltpu.CompilerParams(vmem_limit_bytes=62 << 20),
        name="finish",
    )(back.reduced, back.vector_grads, *handed)


def per_device(*args):
    rows, span, width = args[0].shape
    hidden = args[12].shape[1]
    fits = lax.axis_size("rows") == 8 and lax.axis_size("seq") == 4
    if not fits or (rows, span, width, hidden) != (2, 256, 512, 2048) or args[1].shape != args[0].shape:
        return ring_device(*args)
    matrices, vectors = args[4:14], args[14:23]
    kept = forward_call(args[0], args[1], args[2], args[3], matrices, vectors, args[23], HEADS)
    back = backward_call(kept, matrices, vectors, HEADS)
    return tuple(finish_call(back, hidden))


def solution(mesh):
    placed = (
        P("rows", "seq", None),
        P("rows", "seq", None),
        P("rows", None),
        P("rows", None),
        P(),
        P(),
        P(),
        P(),
        P(),
        P(),
        P(),
        P(),
        P(),
        P(),
        P(),
        P(),
        P(),
        P(),
        P(),
        P(),
        P(),
        P(),
        P(),
        P("rows", "seq", None),
    )
    return jax.shard_map(
        per_device,
        mesh=mesh,
        in_specs=placed,
        out_specs=(
            P("rows", "seq", None),
            P("rows", "seq", None),
            P("rows", "seq", None),
            P(),
            P(),
            P(),
            P(),
            P(),
            P(),
            P(),
            P(),
            P(),
            P(),
            P(),
            P(),
            P(),
            P(),
            P(),
            P(),
            P(),
            P(),
            P(),
        ),
        check_vma=False,
    )
```

profile of v0, /device:TPU:0, one launch (start us, length us, event | category | flops | bytes accessed | tf_op | source)
XLA Modules:
  0.0 156.7 jit_solution(13167438561091042968)
XLA Ops:
  0.7 44.2 %forward.1 = (bf16[2,256,512]{2,1,0:T(8,128)(2,1)}, bf16[1024,512]{1,0:T(8,128)(2,1)}, bf16[1024,512]{1,0:T(8,128)(2,1)}, bf16[2,8,1024,256]{3,2,1,0:T(8,128)(2,...) custom-call(bf16[2,256,512]{2,1,0:T(8,128)(2,1)} %refs_0_.1, ...), custom_call_target="tpu_custom_call" | custom-call | tf_op jit(solution)/shard_map/forward/pallas_call | solution.py:789
  44.8 99.7 %backward.1 = (bf16[2,256,512]{2,1,0:T(8,128)(2,1)}, bf16[16,512,512]{2,1,0:T(8,128)(2,1)}, f32[2,256,512]{2,1,0:T(8,128)}, f32[2,256,512]{2,1,0:T(8,128)}, f32[16,512]{1,0:T(8,128)}) custom-call(bf16[512,2048]{1,0:T(8,128)(2,1)} %get-tuple-element.49.refs_0_, bf16[512,512]{1,0:T(8,128)(2,1)} %get-tuple-element.50.refs_1_, ...), custom_call_target="tpu_custom_call" | custom-call | tf_op jit(solution)/shard_map/backward/pallas_call | solution.py:1274
  144.6 11.9 %finish.1 = (bf16[2,256,512]{2,1,0:T(8,128)(2,1)}, f32[2,256,512]{2,1,0:T(8,128)}, f32[2,256,512]{2,1,0:T(8,128)}, f32[512,512]{1,0:T(8,128)}, f32[512,512]{1,0:...) custom-call(bf16[16,512,512]{2,1,0:T(8,128)(2,1)} %get-tuple-element, ...), custom_call_target="tpu_custom_call" | custom-call | tf_op jit(solution)/shard_map/finish/pallas_call | solution.py:1327
where the time goes:
time: 157 us
  Pallas kernels  156 us (99%)
    pallas_call x1, Pallas kernels, backward_call(): pl.pallas_call(functools.partial(backward_kernel, heads), out_shape=list(...  99.7 us
    pallas_call x1, Pallas kernels, forward_call(): pl.pallas_call(functools.partial(forward_kernel, heads), out_shape=list(o...  44.2 us
    pallas_call x1, Pallas kernels, finish_call(): pl.pallas_call(finish_kernel, out_shape=shapes + [s((width,), f32)] * 9,...  11.9 us

commit v1 on v0

--- a/solution.py
+++ b/solution.py
@@ -516,7 +516,7 @@
     two_hat: object
     two_rstd: object
     active: object
-    upward_grad: object
+    upward_slope: object
     branch_grad: object
     two_grad: object
     sums: object
@@ -532,12 +532,12 @@
     mem_key: object
     mem_value_t: object
     wide: object
-    slope: object
     one: object
     two: object
     value_turned: object
     mem_value_turned: object
     grads: object
+    up: object
 
 FORWARD_NAMES = ForwardIn._fields + ForwardOut._fields
 MATRICES = ForwardIn._fields[4:14]
@@ -661,10 +661,10 @@
         attend_forward(first_block, count, keys, key, value_t, r.query_z, seen, r.scores, r.kept, kept_out, kept_sem, out_t, inverse, heads)
 
     attend(0, 1, length // 2, r.key, r.value_t, r.seen_self, hbm.self_kept, r.self_out, r.self_inverse)
+    attend(1, 1, length, r.key, r.value_t, r.seen_self, hbm.self_kept, r.self_out, r.self_inverse)
     m_side.wait()
     m_pass.start()
     g_side.start()
-    attend(1, 1, length, r.key, r.value_t, r.seen_self, hbm.self_kept, r.self_out, r.self_inverse)
     loads.self_output.wait()
     vec = [getattr(r, k)[...].reshape(1, width) for k in VECTORS]
     part = 128
@@ -711,20 +711,32 @@
     pieces = r.ffn_in.shape[1] // 512
     r.wide[...] = jnp.zeros_like(r.wide)
 
+    halves = [pl.ds(half * (tokens // 2), tokens // 2) for half in range(2)]
+
+    def up(j, half):
+        r.up[half] = dot(r.two_low[halves[half]], r.ffn_in[:, pl.ds(mult(j * 512, 512), 512)])
+
+    def down(j, half):
+        at, cols = halves[half], pl.ds(mult(j * 512, 512), 512)
+        u = r.up[half]
+        square = u * u
+        t = jnp.tanh(u * (c0 + (c0 * 0.044715) * square))
+        rise = 0.5 + 0.5 * t
+        active = (u * rise).astype(bf16)
+        r.active[at, cols] = active
+        r.upward_slope[at, cols] = (rise + u * (rise * (1.0 - t)) * (c0 + (3 * 0.044715 * c0) * square)).astype(bf16)
+        r.wide[at] += dot(active, r.ffn_out[cols, :])
+
+    up(0, 0)
+
     @pl.loop(0, pieces)
     def _(j):
-        cols = pl.ds(mult(j * 512, 512), 512)
-        for half in range(2):
-            at = pl.ds(half * (tokens // 2), tokens // 2)
-            u = dot(r.two_low[at], r.ffn_in[:, cols])
-            square = u * u
-            t = jnp.tanh(c0 * u * (1.0 + 0.044715 * square))
-            active = (0.5 * u * (1.0 + t)).astype(bf16)
-            r.active[at, cols] = active
-            r.slope[at, cols] = (0.5 * (1.0 + t) + (0.5 * c0) * u * (1.0 - t * t) * (1.0 + (3 * 0.044715) * square)).astype(bf16)
-            r.wide[at] += dot(active, r.ffn_out[cols, :])
-
-    emit(*ForwardOut._fields[17:18])
+        up(j, 1)
+        down(j, 0)
+        up(jnp.minimum(j + 1, pieces - 1), 0)
+        down(j, 1)
+
+    emit(*ForwardOut._fields[17:19])
     g_own.wait()
     g_side.wait()
     r.sums[...] = jnp.zeros_like(r.sums)
@@ -748,15 +760,6 @@
 
     emit(*ForwardOut._fields[:1], *ForwardOut._fields[19:])
 
-    @pl.loop(0, pieces)
-    def _(j):
-        cols = pl.ds(mult(j * 512, 512), 512)
-        for half in range(2):
-            at = pl.ds(half * (tokens // 2), tokens // 2)
-            grad = dot_t(r.branch_grad[at], r.ffn_out[cols, :])
-            r.upward_grad[at, cols] = (grad * r.slope[at, cols].astype(f32)).astype(bf16)
-
-    emit(*ForwardOut._fields[18:19])
     for copy in outs:
         copy.wait()
 
@@ -775,14 +778,14 @@
         self_q=s((blocks, span, width), bf16), cross_q=s((blocks, span, width), bf16),
         one_low=s((tokens, width), bf16), one_hat=s(*wide), one_rstd=s((tokens, 128), f32),
         two_low=s((tokens, width), bf16), two_hat=s(*wide), two_rstd=s((tokens, 128), f32),
-        active=s((tokens, hidden), bf16), upward_grad=s((tokens, hidden), bf16), branch_grad=s((tokens, width), bf16),
+        active=s((tokens, hidden), bf16), upward_slope=s((tokens, hidden), bf16), branch_grad=s((tokens, width), bf16),
         two_grad=s(*wide), sums=s((3, 8, width), f32))
     turned = ((width, length), bf16)
     scratch = ForwardScratch(key=full, value_t=turned, query_z=((blocks, heads, 128, span), bf16),
         seen_self=seen, seen_cross=seen, scores=((2, length, span), f32),
         kept=((4, length, span), bf16), mem_key=full, mem_value_t=turned,
-        wide=wide, slope=((tokens, hidden), bf16), one=wide, two=wide,
-        value_turned=((width, width), bf16), mem_value_turned=((width, width), bf16), grads=((blocks, span, width), bf16))
+        wide=wide, one=wide, two=wide,
+        value_turned=((width, width), bf16), mem_value_turned=((width, width), bf16), grads=((blocks, span, width), bf16), up=((2, tokens // 2, 512), f32))
     held = [((8, 128), f32) if k in ForwardOut._fields[3:5] else (o.shape, o.dtype) for k, o in zip(ForwardOut._fields, outs)]
     held = [(m.shape, m.dtype) for m in matrices] + held + list(scratch)
     dma = pltpu.SemaphoreType.DMA
@@ -796,43 +799,43 @@
         name="forward",
     )(target, memory, target_segments, memory_segments, *matrices, *vectors, cotangent))
 
-CLASSES = (1, 4, 0, 1, 4, 4, 0, 5, 1, 4, 1, 1, 3, 0, 1, 0)
+CLASSES = (0, 4, 0, 1, 1, 1, 0, 0, 2, 4, 1, 4, 1, 1, 4, 1)
 PLAN = (
     (0,),
     (19, 1),
+    (2,),
+    (3,),
+    (1, 0, 2, 4),
+    (3, 5),
+    (6,),
+    (7,),
+    (4, 5),
+    (19, 1, 7, 6),
+    (8,),
     (),
     (),
+    (3, 1, 0, 8),
     (2, 4),
-    (0,),
-    (1, 3, 6),
-    (7,),
-    (2, 4, 3, 6, 7),
-    (19, 1, 5),
     (),
+    (1, 7, 5),
+    (9, 0),
+    (10, 8),
+    (11, 2),
+    (16, 1, 6, 9, 3, 7, 10, 0),
+    (11,),
+    (18, 1, 4),
+    (12, 2),
+    (16, 3, 6, 5, 8),
+    (18, 7, 0),
+    (12, 1, 9, 10, 2, 4),
+    (3, 6),
+    (7, 0, 11, 5, 8),
     (),
-    (),
-    (2, 1, 5, 0),
-    (4, 3),
-    (7, 1, 6),
-    (2, 4, 8, 1),
-    (5,),
-    (7, 6),
-    (0, 1, 2, 8),
-    (16, 4, 9, 3),
-    (),
-    (18, 5, 11, 7, 10),
-    (12,),
-    (6,),
-    (16, 8, 18, 7, 4, 9, 1, 2, 11, 0, 10, 3),
-    (12, 7, 5, 8, 6),
-    (2, 1, 3, 0),
-    (9,),
-    (16, 18, 4, 12),
-    (7, 13),
-    (1, 8),
-    (14, 6),
-    (17, 18, 2, 3, 1, 13, 11, 14, 0),
-    (15, 9, 10, 5, 4, 17, 2, 15, 12, 13, 7, 8, 14, 6, 5, 11, 18, 10, 3, 0, 9, 2, 4, 8, 17, 5, 12, 11, 2, 15, 18, 13, 10, 14, 8, 3, 5, 7, 11, 0, 13, 6, 10, 9, 14, 7, 11, 15, 4, 13, 12, 10, 14, 8, 11, 4, 3, 15, 13, 10, 14, 5, 3, 15, 0, 13, 9, 14, 5, 6, 0, 15, 12, 8, 9, 11, 6, 13, 15, 12, 10, 8, 14, 9, 11, 13, 15, 12, 11, 13, 9, 10, 9, 12, 15, 10, 14, 12, 15, 14),
+    (1, 13, 10),
+    (14, 16),
+    (15, 18, 9, 2),
+    (17, 3, 13, 7, 6, 14, 4),
+    (15, 12, 0, 8, 1, 18, 11, 5, 17, 10, 1, 9, 13, 2, 14, 3, 7, 12, 6, 4, 15, 18, 13, 11, 0, 5, 8, 10, 3, 15, 14, 12, 6, 4, 0, 18, 8, 17, 13, 9, 5, 10, 0, 2, 4, 15, 14, 7, 12, 11, 5, 8, 13, 10, 3, 15, 12, 2, 6, 9, 3, 2, 7, 8, 13, 15, 4, 14, 10, 12, 11, 9, 7, 8, 13, 4, 15, 6, 5, 14, 11, 12, 9, 6, 13, 5, 10, 14, 15, 11, 10, 12, 9, 14, 12, 13, 9, 11, 13, 15, 11, 14, 15, 14),
 )
 
 class Reduction:
@@ -924,7 +927,8 @@
     active: object
     branch_grad: object
     two_low: object
-    upward_grad: object
+    upward_slope: object
+    ffn_out: object
     ffn_in: object
     two_grad: object
     two_hat: object
@@ -1019,7 +1023,15 @@
         if c < 4:
             r.block[c] = t_dot(r.active[:, pl.ds(c * 512, 512)], r.branch_grad[...]).astype(bf16)
         else:
-            r.block[c] = t_dot(r.two_low[...], r.upward_grad[:, pl.ds((c - 4) * 512, 512)]).astype(bf16)
+            r.block[c] = t_dot(r.two_low[...], r.upward_slope[:, pl.ds((c - 4) * 512, 512)]).astype(bf16)
+
+    def upward_gradient():
+        @pl.loop(0, r.upward_slope.shape[1] // 512)
+        def _(j):
+            cols = pl.ds(mult(j * 512, 512), 512)
+            for b in range(blocks):
+                grad = dot_t(r.branch_grad[block_at(b)], r.ffn_out[cols, :])
+                r.upward_slope[block_at(b), cols] = (grad * r.upward_slope[block_at(b), cols].astype(f32)).astype(bf16)
 
     vec = [getattr(hbm, k)[...].reshape(1, width) for k in VECTORS]
     part = 128
@@ -1186,7 +1198,8 @@
     need(loads.active, loads.branch_grad)
     for c in range(8):
         if c == 4:
-            need(loads.two_low, loads.upward_grad)
+            need(loads.two_low, loads.upward_slope, loads.ffn_out)
+            upward_gradient()
         ffn_block(c)
         red.poll()
     need(loads.ffn_in, loads.two_grad)
@@ -1194,7 +1207,7 @@
     @pl.loop(0, tokens // 128)
     def _(i):
         at = pl.ds(mult(i * 128, 128), 128)
-        r.two_grad[at] += dot_t(r.upward_grad[at], r.ffn_in[...])
+        r.two_grad[at] += dot_t(r.upward_slope[at], r.ffn_in[...])
     red.poll()
     need(loads.two_hat, loads.two_rstd, loads.one_hat, loads.one_rstd, loads.cross_output, loads.cross_out, loads.cross_inverse)
     norm_back(r.two_grad, r.two_hat, r.two_rstd, vec[5], vec[1], lambda i: r.one_hat[pl.ds(mult(i * part, part), part)] * vec[3] + vec[4], 0)

time: 157 us -> 147 us (0.936)
  Pallas kernels: 156 us -> 146 us
    pallas_call x1, Pallas kernels: 44.2 us -> 39.3 us  [forward_call(): pl.pallas_call(functools.partial(forward_kernel, heads), out_shape=list(o...]
    pallas_call x1, Pallas kernels: 99.7 us -> 95.2 us  [backward_call(): pl.pallas_call(functools.partial(backward_kernel, heads), out_shape=list(...]
where the time goes in v1:
time: 147 us
  Pallas kernels  146 us (99%)
    pallas_call x1, Pallas kernels, backward_call(): pl.pallas_call(functools.partial(backward_kernel, heads), out_shape=list(...  95.2 us
    pallas_call x1, Pallas kernels, forward_call(): pl.pallas_call(functools.partial(forward_kernel, heads), out_shape=list(o...  39.3 us
    pallas_call x1, Pallas kernels, finish_call(): pl.pallas_call(finish_kernel, out_shape=shapes + [s((width,), f32)] * 9,...  11.9 us

profile of v1, /device:TPU:0, one launch (start us, length us, event | category | flops | bytes accessed | tf_op | source)
XLA Modules:
  0.0 147.2 jit_solution(17430231000984670633)
XLA Ops:
  0.7 39.3 %forward.1 = (bf16[2,256,512]{2,1,0:T(8,128)(2,1)}, bf16[1024,512]{1,0:T(8,128)(2,1)}, bf16[1024,512]{1,0:T(8,128)(2,1)}, bf16[2,8,1024,256]{3,2,1,0:T(8,128)(2,...) custom-call(bf16[2,256,512]{2,1,0:T(8,128)(2,1)} %refs_0_.1, ...), custom_call_target="tpu_custom_call" | custom-call | tf_op jit(solution)/shard_map/forward/pallas_call | solution.py:792
  39.9 95.2 %backward.1 = (bf16[2,256,512]{2,1,0:T(8,128)(2,1)}, bf16[16,512,512]{2,1,0:T(8,128)(2,1)}, f32[2,256,512]{2,1,0:T(8,128)}, f32[2,256,512]{2,1,0:T(8,128)}, f32[16,512]{1,0:T(8,128)}) custom-call(bf16[512,2048]{1,0:T(8,128)(2,1)} %get-tuple-element.49.refs_0_, bf16[512,512]{1,0:T(8,128)(2,1)} %get-tuple-element.50.refs_1_, ...), custom_call_target="tpu_custom_call" | custom-call | tf_op jit(solution)/shard_map/backward/pallas_call | solution.py:1287
  135.1 11.9 %finish.1 = (bf16[2,256,512]{2,1,0:T(8,128)(2,1)}, f32[2,256,512]{2,1,0:T(8,128)}, f32[2,256,512]{2,1,0:T(8,128)}, f32[512,512]{1,0:T(8,128)}, f32[512,512]{1,0:...) custom-call(bf16[16,512,512]{2,1,0:T(8,128)(2,1)} %get-tuple-element, ...), custom_call_target="tpu_custom_call" | custom-call | tf_op jit(solution)/shard_map/finish/pallas_call | solution.py:1340

commit v2 on v1

--- a/solution.py
+++ b/solution.py
@@ -1308,7 +1308,8 @@
     for out, block in zip(outs, FINISH_BLOCK):
         places[block] = out
     loads = [pltpu.make_async_copy(reduced.at[i], low.at[i], load_sem.at[i]) for i in range(count)]
-    for copy in loads:
+    ahead = 4
+    for copy in loads[:ahead]:
         copy.start()
     arrive = [pltpu.make_async_copy(a, b, sem.at[i]) for i, (a, b) in enumerate(zip((output, target_grad, memory_grad, vector_grads), (*between, vec)))]
     leave = [pltpu.make_async_copy(a, b, sem.at[4 + i]) for i, (a, b) in enumerate(zip(between, handed))]
@@ -1318,6 +1319,8 @@
     for i, copy in enumerate(copies):
         if i >= slots:
             copies[i - slots].wait()
+        if i + ahead < count:
+            loads[i + ahead].start()
         loads[i].wait()
         stage[i % slots] = low[i].astype(f32)
         copy.start()

time: 147 us -> 147 us (level)
  no operation moved by 1% of the time
where the time goes in v2:
time: 147 us
  Pallas kernels  146 us (99%)
    pallas_call x1, Pallas kernels, backward_call(): pl.pallas_call(functools.partial(backward_kernel, heads), out_shape=list(...  95.2 us
    pallas_call x1, Pallas kernels, forward_call(): pl.pallas_call(functools.partial(forward_kernel, heads), out_shape=list(o...  39.3 us
    pallas_call x1, Pallas kernels, finish_call(): pl.pallas_call(finish_kernel, out_shape=shapes + [s((width,), f32)] * 9,...  11.2 us

profile of v2, /device:TPU:0, one launch (start us, length us, event | category | flops | bytes accessed | tf_op | source)
XLA Modules:
  0.0 146.5 jit_solution(13970094251140608090)
XLA Ops:
  0.7 39.3 %forward.1 = (bf16[2,256,512]{2,1,0:T(8,128)(2,1)}, bf16[1024,512]{1,0:T(8,128)(2,1)}, bf16[1024,512]{1,0:T(8,128)(2,1)}, bf16[2,8,1024,256]{3,2,1,0:T(8,128)(2,...) custom-call(bf16[2,256,512]{2,1,0:T(8,128)(2,1)} %refs_0_.1, ...), custom_call_target="tpu_custom_call" | custom-call | tf_op jit(solution)/shard_map/forward/pallas_call | solution.py:792
  39.9 95.2 %backward.1 = (bf16[2,256,512]{2,1,0:T(8,128)(2,1)}, bf16[16,512,512]{2,1,0:T(8,128)(2,1)}, f32[2,256,512]{2,1,0:T(8,128)}, f32[2,256,512]{2,1,0:T(8,128)}, f32[16,512]{1,0:T(8,128)}) custom-call(bf16[512,2048]{1,0:T(8,128)(2,1)} %get-tuple-element.49.refs_0_, bf16[512,512]{1,0:T(8,128)(2,1)} %get-tuple-element.50.refs_1_, ...), custom_call_target="tpu_custom_call" | custom-call | tf_op jit(solution)/shard_map/backward/pallas_call | solution.py:1287
  135.1 11.2 %finish.1 = (bf16[2,256,512]{2,1,0:T(8,128)(2,1)}, f32[2,256,512]{2,1,0:T(8,128)}, f32[2,256,512]{2,1,0:T(8,128)}, f32[512,512]{1,0:T(8,128)}, f32[512,512]{1,0:...) custom-call(bf16[16,512,512]{2,1,0:T(8,128)(2,1)} %get-tuple-element, ...), custom_call_target="tpu_custom_call" | custom-call | tf_op jit(solution)/shard_map/finish/pallas_call | solution.py:1343

commit v3 on v2

--- a/solution.py
+++ b/solution.py
@@ -644,17 +644,17 @@
     project_self(me_s)
     x_core.wait()
     project_self(other_core)
+    m_own.wait()
+    project_cross(me_s)
+    m_core.wait()
+    project_cross(other_core)
     x_side.wait()
     x_pass.start()
     m_side.start()
     queries(lambda b: r.target_all[place(2 * b + core)], r.self_query, r.self_q)
     project_self(other_side)
-    m_own.wait()
-    project_cross(me_s)
     x_pass.wait()
     project_self(other_side + 1 - 2 * core)
-    m_core.wait()
-    project_cross(other_core)
     emit(*ForwardOut._fields[1:2], *ForwardOut._fields[9:10])
 
     def attend(first_block, count, keys, key, value_t, seen, kept_out, out_t, inverse):
@@ -1011,7 +1011,6 @@
     barrier = pltpu.get_barrier_semaphore()
     for to in red.partners():
         pl.semaphore_signal(barrier, inc=1, device_id=to, device_id_type=MESH)
-    pl.semaphore_wait(barrier, 5)
 
     def block_at(b):
         return pl.ds(b * span, span)
@@ -1201,6 +1200,8 @@
             need(loads.two_low, loads.upward_slope, loads.ffn_out)
             upward_gradient()
         ffn_block(c)
+        if c == 0:
+            pl.semaphore_wait(barrier, 5)
         red.poll()
     need(loads.ffn_in, loads.two_grad)
 

time: 147 us -> 146 us (level)
  no operation moved by 1% of the time
where the time goes in v3:
time: 146 us
  Pallas kernels  145 us (99%)
    pallas_call x1, Pallas kernels, backward_call(): pl.pallas_call(functools.partial(backward_kernel, heads), out_shape=list(...  95.1 us
    pallas_call x1, Pallas kernels, forward_call(): pl.pallas_call(functools.partial(forward_kernel, heads), out_shape=list(o...  38.9 us
    pallas_call x1, Pallas kernels, finish_call(): pl.pallas_call(finish_kernel, out_shape=shapes + [s((width,), f32)] * 9,...  11.2 us

profile of v3, /device:TPU:0, one launch (start us, length us, event | category | flops | bytes accessed | tf_op | source)
XLA Modules:
  0.0 146.1 jit_solution(17068577381801109127)
XLA Ops:
  0.7 38.9 %forward.1 = (bf16[2,256,512]{2,1,0:T(8,128)(2,1)}, bf16[1024,512]{1,0:T(8,128)(2,1)}, bf16[1024,512]{1,0:T(8,128)(2,1)}, bf16[2,8,1024,256]{3,2,1,0:T(8,128)(2,...) custom-call(bf16[2,256,512]{2,1,0:T(8,128)(2,1)} %refs_0_.1, ...), custom_call_target="tpu_custom_call" | custom-call | tf_op jit(solution)/shard_map/forward/pallas_call | solution.py:792
  39.6 95.1 %backward.1 = (bf16[2,256,512]{2,1,0:T(8,128)(2,1)}, bf16[16,512,512]{2,1,0:T(8,128)(2,1)}, f32[2,256,512]{2,1,0:T(8,128)}, f32[2,256,512]{2,1,0:T(8,128)}, f32[16,512]{1,0:T(8,128)}) custom-call(bf16[512,2048]{1,0:T(8,128)(2,1)} %get-tuple-element.49.refs_0_, bf16[512,512]{1,0:T(8,128)(2,1)} %get-tuple-element.50.refs_1_, ...), custom_call_target="tpu_custom_call" | custom-call | tf_op jit(solution)/shard_map/backward/pallas_call | solution.py:1288
  134.7 11.2 %finish.1 = (bf16[2,256,512]{2,1,0:T(8,128)(2,1)}, f32[2,256,512]{2,1,0:T(8,128)}, f32[2,256,512]{2,1,0:T(8,128)}, f32[512,512]{1,0:T(8,128)}, f32[512,512]{1,0:...) custom-call(bf16[16,512,512]{2,1,0:T(8,128)(2,1)} %get-tuple-element, ...), custom_call_target="tpu_custom_call" | custom-call | tf_op jit(solution)/shard_map/finish/pallas_call | solution.py:1344
